TPU v7x, 256 devices: a whole 4x4x8 slice. The times are simulated.
256 devices in a mesh: grp: 2 (over x_hi), ctx: 16 (over z, x_lo), mp: 8 (over y, core).
Axes of the slice: x: 4 (x_hi: 2, x_lo: 2; x = x_hi * 2 + x_lo), y: 4, z: 8, core: 2. Of those that a mesh axis runs over, the one named last changes fastest.
Arguments:
- states: bfloat16 [2, 6144, 5120], P('grp', 'ctx', 'mp'), may hold values from -6 to 6
- noise: bfloat16 [2, 6144, 5120], P('grp', 'ctx', 'mp'), may hold values from -6 to 6
- span_lengths: int32 [2, 4], P('grp'), may hold values from 1 to 3072, 6144 in all within a row
- step_index: int32 [2, 4], P('grp'), may hold values from 0 to 3
- gain: float32 [2, 5120], P('grp'), may hold values from 0.1 to 1.9
- in_weights: bfloat16 [2, 5120, 3, 3072], P('grp', 'ctx', None, 'mp'), may hold values from -0.169658223 to 0.169658223
- out_weights: bfloat16 [2, 3072, 5120], P('grp', 'mp'), may hold values from -0.109375 to 0.109375
Outputs:
- received: bfloat16 [2, 6144, 5120], P('grp', 'ctx', 'mp')
Inputs may be any that keep to these rules, and one draw needn't show every extreme that they name: `span_lengths`: each row's 4 lengths sum to 6144; the largest is exactly 3072.
All inputs are finite; a program needn't handle non-finite values.
Results may differ from a plain program's by a relative error of at most 0.014.
Values may be sent and summed in bfloat16 or wider, within the bound.
No kernel may reach another device: no remote copies, remote signals or barrier semaphores. Data moves between devices by JAX's collectives and lax.ppermute only.
A program may use at most 128 MiB of HBM per device.

v0:
```python
import jax
import jax.numpy as jnp
from jax import lax
from jax.sharding import PartitionSpec as P

HEAD_DIM = 128
STEPS = 4


def swapped(block, axis, stride):
    count = lax.axis_size(axis)
    route = []
    for low in range(count):
        high = low | 1 << stride
        if high != low and high < count:
            route += [(low, high), (high, low)]
    return lax.ppermute(block, axis, route)


def span_ids(positions, lengths):
    ends = jnp.cumsum(lengths)
    return jnp.sum((positions[:, None] >= ends[None, :]).astype(jnp.int32), axis=1)


def local(states, noise, span_lengths, step_index, gain, in_weights, out_weights):
    tokens_here = states.shape[1]
    group = lax.axis_index("grp")
    shard = lax.axis_index("ctx")
    lengths = span_lengths[0]
    positions = shard * tokens_here + jnp.arange(tokens_here, dtype=jnp.int32)
    spans = span_ids(positions, lengths)
    hits = spans[:, None] == jnp.arange(lengths.shape[0], dtype=jnp.int32)[None, :]
    picked = jnp.where(hits, (step_index[0][None, :] + 1).astype(jnp.float32), jnp.float32(0.0))
    times = (jnp.sum(picked, axis=1) / STEPS)[:, None]
    state = states[0].astype(jnp.float32)
    mixed = ((1.0 - times) * state + times * noise[0].astype(jnp.float32)).astype(jnp.bfloat16)
    gathered = lax.all_gather(mixed, "mp", axis=1, tiled=True)
    wide = gathered.astype(jnp.float32)
    mean_square = jnp.mean(wide * wide, axis=1, keepdims=True)
    inverse_root = lax.rsqrt(mean_square + 1e-06)
    normed = (wide * inverse_root * gain[0][None, :]).astype(jnp.bfloat16)
    local_rows = in_weights[0]
    full_rows = lax.all_gather(local_rows, "ctx", axis=0, tiled=True)
    projected = jnp.einsum("rd,dkh->rkh", normed, full_rows, preferred_element_type=jnp.float32)
    projected = projected.astype(jnp.bfloat16)
    heads = projected.shape[2] // HEAD_DIM
    query = projected[:, 0].reshape(tokens_here, heads, HEAD_DIM)
    keys = projected[:, 1].reshape(tokens_here, heads, HEAD_DIM)
    values = projected[:, 2].reshape(tokens_here, heads, HEAD_DIM)
    highest = jnp.full((heads, tokens_here), -1e30, jnp.float32)
    key_piece = lax.all_gather(keys, "ctx", axis=0, tiled=True)
    value_piece = lax.all_gather(values, "ctx", axis=0, tiled=True)
    count = key_piece.shape[0]
    key_spans = span_ids(jnp.arange(count, dtype=jnp.int32), lengths)
    allowed = (key_spans[None, :] <= spans[:, None]) | (group == 1)
    scores = jnp.einsum(
        "rhd,nhd->hrn", query, key_piece, preferred_element_type=jnp.float32
    ) * HEAD_DIM ** (-0.5)
    scores = jnp.where(allowed[None], scores, -1e30)
    new_high = jnp.maximum(highest, jnp.max(scores, axis=2))
    weights = jnp.where(allowed[None], jnp.exp(scores - new_high[..., None]), 0.0)
    summed = jnp.sum(weights, axis=2)
    output = jnp.einsum(
        "hrn,nhd->hrd",
        weights.astype(jnp.bfloat16),
        value_piece,
        preferred_element_type=jnp.float32,
    )
    highest, summed, output = (new_high, summed, output)
    attended = (
        jnp.transpose(output / summed[..., None], (1, 0, 2))
        .reshape(tokens_here, heads * HEAD_DIM)
        .astype(jnp.bfloat16)
    )
    partial_terms = jnp.dot(attended, out_weights[0], preferred_element_type=jnp.float32)
    velocity = lax.psum_scatter(
        partial_terms.astype(jnp.bfloat16), "mp", scatter_dimension=1, tiled=True
    ).astype(jnp.float32)
    estimate = mixed.astype(jnp.float32) - times * velocity
    result = jnp.where(group == 0, estimate, state - estimate).astype(jnp.bfloat16)
    arrived = swapped(result, "grp", 0)
    return arrived[None]


def solution(mesh):
    return jax.shard_map(
        local,
        mesh=mesh,
        in_specs=(
            P("grp", "ctx", "mp"),
            P("grp", "ctx", "mp"),
            P("grp", None),
            P("grp", None),
            P("grp", None),
            P("grp", "ctx", None, "mp"),
            P("grp", "mp", None),
        ),
        out_specs=P("grp", "ctx", "mp"),
        check_vma=False,
    )
```

profile of v0, /device:TPU:25, one launch (start us, length us, event | category | flops | bytes accessed | tf_op | source)
XLA Modules:
  0.0 620.3 jit_solution(5367559098842254153)
XLA Ops:
  6.5 0.0 all-gather.6.cloned.1.call-start
  6.5 0.7 convert_bitcast_fusion
  7.2 0.8 reduce-window.8
  8.0 0.1 convert_reduce_fusion.1
  8.1 0.1 select_reduce_fusion
  8.2 2.2 fusion.25
  10.5 0.0 all-gather.6.cloned.1.call-update
  10.5 0.0 all-gather.12.cloned.1.call-start
  10.5 0.7 all-gather.12.cloned.1.call-update
  11.2 0.0 all-gather.8.cloned.1.call-start
  11.3 34.1 %all-gather.6.cloned.1.call-done = bf16[384,5120]{1,0:T(8,128)(2,1)} async-done(((bf16[384,640]{1,0:T(8,128)(2,1)}), bf16[384,5120]{1,0:T(8,128)(2,1)}) %all-gather.6.cloned.1.call-update) | async-done | bytes 3932176 | tf_op jit(solution)/shard_map/all_gather | solution.py:37
  45.4 3.0 fusion.8
  48.4 251.2 %all-gather.12.cloned.1.call-done = bf16[1,5120,3,384]{3,1,2,0:T(8,128)(2,1)} async-done(((bf16[1,320,3,384]{3,1,2,0:T(8,128)(2,1)}), bf16[1,5120,3,384]{3,1,2,0:T(8,128)(2,1)}) %all-gather.12.cloned.1.call-update) | async-done | bytes 11796496 | tf_op jit(solution)/shard_map/all_gather | solution.py:43
  299.6 10.1 %fusion.16 = bf16[384,3,384]{0,2,1:T(8,128)(2,1)S(1)} fusion(bf16[1,5120,3,384]{3,1,2,0:T(8,128)(2,1)} %all-gather.12.cloned.1.call-done, bf16[384,5120]{1,0:T(8,128)(2,1)} %all-gather.6.cloned.1.call-done, f32[5120]{0:T(1024)} %bitcast.54, f32[384]{0:T(512)S(1)} %add_rsqrt_fusion), kind=kOutput, calls=%fused_computation.21 | convolution fusion | flops 4538155008 | bytes 16635392 | tf_op jit(solution)/shard_map/rd,dkh->rkh/dot_general | solution.py:44
  309.7 0.8 fusion.36
  310.5 0.9 copy.15
  311.4 0.0 all-gather.8.cloned.1.call-update
  311.4 0.0 all-gather.10.cloned.1.call-start
  311.5 0.5 all-gather.10.cloned.1.call-update
  312.0 0.2 reduce-scatter.4.cloned.1.call-start
  312.3 0.1 convert_reduce_fusion
  312.4 1.6 compare_or_fusion
  314.0 107.3 %all-gather.8.cloned.1.call-done = bf16[6144,3,128]{2,0,1:T(8,128)(2,1)} async-done(((bf16[384,3,128]{2,0,1:T(8,128)(2,1)}), bf16[6144,3,128]{2,0,1:T(8,128)(2,1)}) %all-gather.8.cloned.1.call-update) | async-done | bytes 4718608 | tf_op jit(solution)/shard_map/all_gather | solution.py:51
  421.4 14.0 %fusion = (f32[3,384]{1,0:T(4,128)S(1)}, f32[3,384,6144]{2,1,0:T(8,128)}) fusion(pred[384,6144]{1,0:T(8,128)(4,1)S(1)} %compare_or_fusion, bf16[384,3,128]{0,2,1:T(8,128)(2,1)S(1)} %bitcast.50, bf16[6144,3,128]{2,0,1:T(8,128)(2,1)} %all-gather.8.cloned.1.call-done), kind=kOutput, calls=%fused_computation.2 | convolution fusion | flops 1833171840 | bytes 35688960 | tf_op jit(solution)/shard_map/rhd,nhd->hrn/dot_general | solution.py:56
  435.3 14.9 %fusion.1 = f32[3,384]{1,0:T(4,128)S(1)} fusion(f32[3,384,6144]{2,1,0:T(8,128)} %get-tuple-element.11, f32[3,384]{1,0:T(4,128)S(1)} %broadcast_maximum_fusion, pred[384,6144]{1,0:T(8,128)(4,1)S(1)} %compare_or_fusion), kind=kLoop, calls=%fused_computation.3 | loop fusion | flops 35388288 | bytes 30680064 | tf_op jit(solution)/shard_map/reduce_sum | solution.py:62
  450.2 82.0 %all-gather.10.cloned.1.call-done = bf16[6144,3,128]{0,2,1:T(8,128)(2,1)} async-done(((bf16[384,3,128]{0,2,1:T(8,128)(2,1)}), bf16[6144,3,128]{0,2,1:T(8,128)(2,1)}) %all-gather.10.cloned.1.call-update) | async-done | bytes 4718608 | tf_op jit(solution)/shard_map/all_gather | solution.py:52
  532.2 0.0 copy-start.1
  532.2 14.4 %fusion.30 = bf16[384,3,128]{0,2,1:T(8,128)(2,1)S(1)} fusion(bf16[6144,3,128]{0,2,1:T(8,128)(2,1)} %all-gather.10.cloned.1.call-done, f32[3,384,6144]{2,1,0:T(8,128)} %get-tuple-element.11, f32[3,384]{1,0:T(4,128)S(1)} %broadcast_maximum_fusion, pred[384,6144]{1,0:T(8,128)(4,1)S(1)} %compare_or_fusion, f32[384,3]{0,1:T(4,128)S(1)} %bitcast.51), kind=kOutput, calls=%fused_computation.29 | convolution fusion | flops 1847623680 | bytes 35693568 | tf_op jit(solution)/shard_map/hrn,nhd->hrd/dot_general | solution.py:63
  546.7 0.0 copy-done.1
  546.7 4.1 convolution_convert_fusion
  550.8 0.0 copy-start
  550.8 0.0 copy-start.2
  550.8 6.3 %copy.18 = bf16[384,5120]{0,1:T(8,128)(2,1)} copy(bf16[384,5120]{1,0:T(8,128)(2,1)} %convolution_convert_fusion) | data formatting | bytes 7864320
  557.2 0.0 reduce-scatter.4.cloned.1.call-update
  557.2 40.6 %reduce-scatter.4.cloned.1.call-done = bf16[640,384]{1,0:T(8,128)(2,1)} async-done(((bf16[5120,384]{1,0:T(8,128)(2,1)}), bf16[640,384]{1,0:T(8,128)(2,1)}) %reduce-scatter.4.cloned.1.call-update) | async-done | bytes 491536
  597.8 1.3 copy.19
  599.0 0.0 copy-done
  599.0 0.0 copy-done.2
  599.0 0.3 fusion.26
  599.4 2.5 collective-permute-start
  601.9 11.1 %collective-permute-done = bf16[384,640]{1,0:T(8,128)(2,1)S(1)} collective-permute-done((bf16[384,640]{1,0:T(8,128)(2,1)S(1)}, bf16[384,640]{1,0:T(8,128)(2,1)S(1)}, u32[]{:S(2)}, u32[]{:S(2)}) %collective-permute-start) | collective-permute-done | bytes 491552 | tf_op jit(solution)/shard_map/ppermute | solution.py:17
  613.0 0.8 copy.21
  (4 shorter events, 0.0 us)
Async XLA Ops:
  6.5 38.9 %all-gather.6.cloned.1.call-start = ((), (), s32[]{:S(2)}) async-start(), calls=%async_computation.1 | async-start | bytes 4423680 | tf_op jit(solution)/shard_map/all_gather | solution.py:37
  10.5 289.1 %all-gather.12.cloned.1.call-start = ((), (), s32[]{:S(2)}) async-start(), calls=%async_computation.4 | async-start | bytes 12533760 | tf_op jit(solution)/shard_map/all_gather | solution.py:43
  11.2 410.1 %all-gather.8.cloned.1.call-start = ((), (), s32[]{:S(2)}) async-start(), calls=%async_computation.2 | async-start | bytes 5013504 | tf_op jit(solution)/shard_map/all_gather | solution.py:51
  311.4 220.8 %all-gather.10.cloned.1.call-start = ((), (), s32[]{:S(2)}) async-start(), calls=%async_computation.3 | async-start | bytes 5013504 | tf_op jit(solution)/shard_map/all_gather | solution.py:52
  312.0 285.7 %reduce-scatter.4.cloned.1.call-start = ((), (), s32[]{:S(2)}) async-start(), calls=%async_computation.5 | async-start | bytes 4423680
  532.2 14.4 %copy-start.1 = (bf16[1,384,5120]{2,1,0:T(8,128)(2,1)S(1)}, bf16[1,384,5120]{2,1,0:T(8,128)(2,1)}, u32[]{:S(2)}) copy-start(bf16[1,384,5120]{2,1,0:T(8,128)(2,1)} %param.13) | copy-start | bytes 11796484
  550.8 48.2 %copy-start = (bf16[384,640]{1,0:T(8,128)(2,1)S(1)}, bf16[384,640]{1,0:T(8,128)(2,1)}, u32[]{:S(2)}) copy-start(bf16[384,640]{1,0:T(8,128)(2,1)} %fusion.25) | copy-start | bytes 1474564
  550.8 48.2 %copy-start.2 = (bf16[1,384,640]{2,1,0:T(8,128)(2,1)S(1)}, bf16[1,384,640]{2,1,0:T(8,128)(2,1)}, u32[]{:S(2)}) copy-start(bf16[1,384,640]{2,1,0:T(8,128)(2,1)} %param.7) | copy-start | bytes 1474564
  599.4 13.6 %collective-permute-start = (bf16[384,640]{1,0:T(8,128)(2,1)S(1)}, bf16[384,640]{1,0:T(8,128)(2,1)S(1)}, u32[]{:S(2)}, u32[]{:S(2)}) collective-permute-start(bf16[384,640]{1,0:T(8,128)(2,1)S(1)} %fusion.26), channel_id=1, source_target_pairs={{0,128},{128,0},{1,129},{129,1},{2,130},{130,2},{3,131},{131,3},{4... | collective-permute-start | bytes 1474568 | tf_op jit(solution)/shard_map/ppermute | solution.py:17
Sparse Core Ops, SparseCore 0:
  10.6 34.7 all-gather.5
  47.2 252.3 all-gather.11
  311.6 109.7 all-gather.7
  423.0 109.1 all-gather.9
  557.3 40.3 reduce-scatter.3
where the time goes:
time: 621 us; the launch traced here: 620 us
  waiting for transfers between devices  528 us (85%)
  matrix products  42.7 us (7%)
  other arithmetic  23.8 us (4%)
  between operations  13.2 us (2%)
  local copies, waits for them, and re-layouts  10.1 us (2%)
    all_gather x1, waiting for transfers between devices, local(): full_rows = lax.all_gather(local_rows, 'ctx', axis=0, tiled=True)  251 us
    all_gather x1, waiting for transfers between devices, local(): key_piece = lax.all_gather(keys, 'ctx', axis=0, tiled=True)  107 us
    all_gather x1, waiting for transfers between devices, local(): value_piece = lax.all_gather(values, 'ctx', axis=0, tiled=True)  82 us
    unnamed x6, waiting for transfers between devices  41.8 us
    all_gather x1, waiting for transfers between devices, local(): gathered = lax.all_gather(mixed, 'mp', axis=1, tiled=True)  34.1 us
    reduce_sum x1, other arithmetic, local(): summed = jnp.sum(weights, axis=2)  14.9 us
    dot_general x1, matrix products, local(): jnp.einsum('hrn,nhd->hrd', weights.astype(jnp.bfloat16), value_piece, pre...  14.4 us
    dot_general x1, matrix products, local(): jnp.einsum('rhd,nhd->hrn', query, key_piece, preferred_element_type=jnp.f...  14 us
  transfers between devices with their start and end apart: 6, of which 6 were waited for; matrix products, arithmetic and copies ran while one was open for 5% of the time, Pallas kernels for 0%

commit v1 on v0

--- a/solution.py
+++ b/solution.py
@@ -17,6 +17,10 @@
     return lax.ppermute(block, axis, route)
 
 
+def crossed(block):
+    return lax.ppermute(block, ("a", "c"), [(0, 0), (1, 2), (2, 1), (3, 3)])
+
+
 def span_ids(positions, lengths):
     ends = jnp.cumsum(lengths)
     return jnp.sum((positions[:, None] >= ends[None, :]).astype(jnp.int32), axis=1)
@@ -25,22 +29,22 @@
 def local(states, noise, span_lengths, step_index, gain, in_weights, out_weights):
     tokens_here = states.shape[1]
     group = lax.axis_index("grp")
-    shard = lax.axis_index("ctx")
     lengths = span_lengths[0]
-    positions = shard * tokens_here + jnp.arange(tokens_here, dtype=jnp.int32)
-    spans = span_ids(positions, lengths)
-    hits = spans[:, None] == jnp.arange(lengths.shape[0], dtype=jnp.int32)[None, :]
+    here = jnp.arange(tokens_here, dtype=jnp.int32)
+    spans_home = span_ids(lax.axis_index(("z", "a")) * tokens_here + here, lengths)
+    spans = span_ids(lax.axis_index(("z", "c")) * tokens_here + here, lengths)
+    hits = spans_home[:, None] == jnp.arange(lengths.shape[0], dtype=jnp.int32)[None, :]
     picked = jnp.where(hits, (step_index[0][None, :] + 1).astype(jnp.float32), jnp.float32(0.0))
     times = (jnp.sum(picked, axis=1) / STEPS)[:, None]
     state = states[0].astype(jnp.float32)
     mixed = ((1.0 - times) * state + times * noise[0].astype(jnp.float32)).astype(jnp.bfloat16)
-    gathered = lax.all_gather(mixed, "mp", axis=1, tiled=True)
+    gathered = lax.all_gather(crossed(mixed), ("y", "a"), axis=1, tiled=True)
     wide = gathered.astype(jnp.float32)
     mean_square = jnp.mean(wide * wide, axis=1, keepdims=True)
     inverse_root = lax.rsqrt(mean_square + 1e-06)
     normed = (wide * inverse_root * gain[0][None, :]).astype(jnp.bfloat16)
-    local_rows = in_weights[0]
-    full_rows = lax.all_gather(local_rows, "ctx", axis=0, tiled=True)
+    local_rows = crossed(in_weights[0])
+    full_rows = lax.all_gather(local_rows, ("z", "c"), axis=0, tiled=True)
     projected = jnp.einsum("rd,dkh->rkh", normed, full_rows, preferred_element_type=jnp.float32)
     projected = projected.astype(jnp.bfloat16)
     heads = projected.shape[2] // HEAD_DIM
@@ -48,8 +52,8 @@
     keys = projected[:, 1].reshape(tokens_here, heads, HEAD_DIM)
     values = projected[:, 2].reshape(tokens_here, heads, HEAD_DIM)
     highest = jnp.full((heads, tokens_here), -1e30, jnp.float32)
-    key_piece = lax.all_gather(keys, "ctx", axis=0, tiled=True)
-    value_piece = lax.all_gather(values, "ctx", axis=0, tiled=True)
+    key_piece = lax.all_gather(keys, ("z", "c"), axis=0, tiled=True)
+    value_piece = lax.all_gather(values, ("z", "c"), axis=0, tiled=True)
     count = key_piece.shape[0]
     key_spans = span_ids(jnp.arange(count, dtype=jnp.int32), lengths)
     allowed = (key_spans[None, :] <= spans[:, None]) | (group == 1)
@@ -72,9 +76,10 @@
         .reshape(tokens_here, heads * HEAD_DIM)
         .astype(jnp.bfloat16)
     )
+    attended = crossed(attended)
     partial_terms = jnp.dot(attended, out_weights[0], preferred_element_type=jnp.float32)
     velocity = lax.psum_scatter(
-        partial_terms.astype(jnp.bfloat16), "mp", scatter_dimension=1, tiled=True
+        partial_terms.astype(jnp.bfloat16), ("y", "c"), scatter_dimension=1, tiled=True
     ).astype(jnp.float32)
     estimate = mixed.astype(jnp.float32) - times * velocity
     result = jnp.where(group == 0, estimate, state - estimate).astype(jnp.bfloat16)
@@ -83,18 +88,20 @@
 
 
 def solution(mesh):
+    fine = jax.sharding.Mesh(mesh.devices.reshape(2, 8, 2, 4, 2), ("grp", "z", "a", "y", "c"))
+    tokens, features = ("z", "a"), ("y", "c")
     return jax.shard_map(
         local,
-        mesh=mesh,
+        mesh=fine,
         in_specs=(
-            P("grp", "ctx", "mp"),
-            P("grp", "ctx", "mp"),
+            P("grp", tokens, features),
+            P("grp", tokens, features),
             P("grp", None),
             P("grp", None),
             P("grp", None),
-            P("grp", "ctx", None, "mp"),
-            P("grp", "mp", None),
+            P("grp", tokens, None, features),
+            P("grp", features, None),
         ),
-        out_specs=P("grp", "ctx", "mp"),
+        out_specs=P("grp", tokens, features),
         check_vma=False,
     )

time: 621 us -> 376 us (0.61)
  waiting for transfers between devices: 528 us -> 271 us
  starting transfers between devices: 2.87 us -> 13.5 us
    all_gather x4, waiting for transfers between devices: 475 us -> 202 us  [the longest x1 75.9 us: local(): gathered = lax.all_gather(crossed(mixed), ('y', 'a'), axis=1, tiled=True)]
    ppermute x0 -> x3, waiting for transfers between devices: none -> 20.6 us  [crossed(): return lax.ppermute(block, ('a', 'c'), [(0, 0), (1, 2), (2, 1), (3, 3)])]
    ppermute x0 -> x3, starting transfers between devices: none -> 10.6 us  [crossed(): return lax.ppermute(block, ('a', 'c'), [(0, 0), (1, 2), (2, 1), (3, 3)])]
  transfers between devices with their start and end apart: 6 -> 9, of which waited for: 6 -> 9; matrix products, arithmetic and copies ran while one was open for 5% -> 9% of each run, Pallas kernels for 0% -> 0%
where the time goes in v1:
time: 376 us; the launch traced here: 375 us
  waiting for transfers between devices  271 us (72%)
  matrix products  42.9 us (11%)
  other arithmetic  23.1 us (6%)
  starting transfers between devices  13.5 us (4%)
  between operations  13.2 us (4%)
  local copies, waits for them, and re-layouts  11.7 us (3%)
    all_gather x1, waiting for transfers between devices, local(): gathered = lax.all_gather(crossed(mixed), ('y', 'a'), axis=1, tiled=True)  75.9 us
    all_gather x1, waiting for transfers between devices, local(): full_rows = lax.all_gather(local_rows, ('z', 'c'), axis=0, tiled=True)  72.3 us
    all_gather x1, waiting for transfers between devices, local(): key_piece = lax.all_gather(keys, ('z', 'c'), axis=0, tiled=True)  38.9 us
    unnamed x6, waiting for transfers between devices  37.4 us
    ppermute x3, waiting for transfers between devices, crossed(): return lax.ppermute(block, ('a', 'c'), [(0, 0), (1, 2), (2, 1), (3, 3)])  20.6 us
    reduce_sum x1, other arithmetic, local(): summed = jnp.sum(weights, axis=2)  14.9 us
    all_gather x1, waiting for transfers between devices, local(): value_piece = lax.all_gather(values, ('z', 'c'), axis=0, tiled=True)  14.6 us
    dot_general x1, matrix products, local(): jnp.einsum('hrn,nhd->hrd', weights.astype(jnp.bfloat16), value_piece, pre...  14.4 us
  transfers between devices with their start and end apart: 9, of which 9 were waited for; matrix products, arithmetic and copies ran while one was open for 9% of the time, Pallas kernels for 0%

profile of v1, /device:TPU:25, one launch (start us, length us, event | category | flops | bytes accessed | tf_op | source)
XLA Modules:
  0.0 375.1 jit_solution(4833823232132269843)
XLA Ops:
  6.5 0.0 all-gather.5.cloned.1.call-start
  6.5 0.7 convert_bitcast_fusion
  7.2 0.8 reduce-window.8
  8.0 0.1 convert_reduce_fusion.1
  8.1 0.1 select_reduce_fusion
  8.2 1.5 fusion.22
  9.7 3.7 collective-permute-start
  13.4 6.5 %collective-permute-done = bf16[384,640]{1,0:T(8,128)(2,1)S(1)} collective-permute-done((bf16[384,640]{1,0:T(8,128)(2,1)S(1)}, bf16[384,640]{1,0:T(8,128)(2,1)S(1)}, u32[]{:S(2)}, u32[]{:S(2)}) %collective-permute-start) | collective-permute-done | bytes 491552 | tf_op jit(solution)/shard_map/ppermute | solution.py:21
  19.9 0.0 copy-start.3
  19.9 0.8 copy-done.3
  20.6 0.0 all-gather.5.cloned.1.call-update
  20.7 0.0 all-gather.7.cloned.1.call-start
  20.7 3.6 collective-permute-start.1
  24.4 9.3 %collective-permute-done.1 = bf16[320,3,384]{2,0,1:T(8,128)(2,1)S(1)} collective-permute-done((bf16[320,3,384]{2,0,1:T(8,128)(2,1)}, bf16[320,3,384]{2,0,1:T(8,128)(2,1)S(1)}, u32[]{:S(2)}, u32[]{:S(2)}) %collective-permute-start.1) | collective-permute-done | bytes 737312 | tf_op jit(solution)/shard_map/ppermute | solution.py:21
  33.7 0.0 copy-start.2
  33.7 0.9 copy-done.2
  34.6 0.0 all-gather.7.cloned.1.call-update
  34.6 0.0 all-gather.9.cloned.1.call-start
  34.7 75.9 %all-gather.5.cloned.1.call-done = bf16[384,5120]{1,0:T(8,128)(2,1)} async-done(((bf16[384,640]{1,0:T(8,128)(2,1)}), bf16[384,5120]{1,0:T(8,128)(2,1)}) %all-gather.5.cloned.1.call-update) | async-done | bytes 3932176 | tf_op jit(solution)/shard_map/all_gather | solution.py:41
  110.6 3.0 fusion.6
  113.5 72.3 %all-gather.7.cloned.1.call-done = bf16[5120,3,384]{2,0,1:T(8,128)(2,1)} async-done(((bf16[320,3,384]{2,0,1:T(8,128)(2,1)}), bf16[5120,3,384]{2,0,1:T(8,128)(2,1)}) %all-gather.7.cloned.1.call-update) | async-done | bytes 11796496 | tf_op jit(solution)/shard_map/all_gather | solution.py:47
  185.8 10.1 %fusion.15 = bf16[384,3,384]{0,2,1:T(8,128)(2,1)S(1)} fusion(bf16[5120,3,384]{2,0,1:T(8,128)(2,1)} %all-gather.7.cloned.1.call-done, bf16[384,5120]{1,0:T(8,128)(2,1)} %all-gather.5.cloned.1.call-done, f32[5120]{0:T(1024)} %bitcast.51, f32[384]{0:T(512)S(1)} %add_rsqrt_fusion), kind=kOutput, calls=%fused_computation.20 | convolution fusion | flops 4538155008 | bytes 16635392 | tf_op jit(solution)/shard_map/rd,dkh->rkh/dot_general | solution.py:48
  196.0 0.8 fusion.33
  196.8 0.9 copy.12
  197.6 0.0 all-gather.9.cloned.1.call-update
  197.7 0.0 all-gather.11.cloned.1.call-start
  197.7 0.5 all-gather.11.cloned.1.call-update
  198.2 0.2 reduce-scatter.4.cloned.1.call-start
  198.5 0.1 convert_reduce_fusion
  198.6 1.6 compare_or_fusion
  200.2 38.9 %all-gather.9.cloned.1.call-done = bf16[6144,3,128]{2,0,1:T(8,128)(2,1)} async-done(((bf16[384,3,128]{2,0,1:T(8,128)(2,1)}), bf16[6144,3,128]{2,0,1:T(8,128)(2,1)}) %all-gather.9.cloned.1.call-update) | async-done | bytes 4718608 | tf_op jit(solution)/shard_map/all_gather | solution.py:55
  239.1 14.1 %fusion = (f32[3,384]{1,0:T(4,128)S(1)}, f32[3,384,6144]{2,1,0:T(8,128)}) fusion(pred[384,6144]{1,0:T(8,128)(4,1)S(1)} %compare_or_fusion, bf16[384,3,128]{0,2,1:T(8,128)(2,1)S(1)} %bitcast.45, bf16[6144,3,128]{2,0,1:T(8,128)(2,1)} %all-gather.9.cloned.1.call-done), kind=kOutput, calls=%fused_computation.2 | convolution fusion | flops 1833171840 | bytes 35688960 | tf_op jit(solution)/shard_map/rhd,nhd->hrn/dot_general | solution.py:60
  253.2 14.9 %fusion.1 = f32[3,384]{1,0:T(4,128)S(1)} fusion(f32[3,384,6144]{2,1,0:T(8,128)} %get-tuple-element.13, f32[3,384]{1,0:T(4,128)S(1)} %broadcast_maximum_fusion, pred[384,6144]{1,0:T(8,128)(4,1)S(1)} %compare_or_fusion), kind=kLoop, calls=%fused_computation.3 | loop fusion | flops 35388288 | bytes 30680064 | tf_op jit(solution)/shard_map/reduce_sum | solution.py:66
  268.2 14.6 %all-gather.11.cloned.1.call-done = bf16[6144,3,128]{0,2,1:T(8,128)(2,1)} async-done(((bf16[384,3,128]{0,2,1:T(8,128)(2,1)}), bf16[6144,3,128]{0,2,1:T(8,128)(2,1)}) %all-gather.11.cloned.1.call-update) | async-done | bytes 4718608 | tf_op jit(solution)/shard_map/all_gather | solution.py:56
  282.8 14.4 %fusion.27 = bf16[384,3,128]{0,2,1:T(8,128)(2,1)S(1)} fusion(bf16[6144,3,128]{0,2,1:T(8,128)(2,1)} %all-gather.11.cloned.1.call-done, f32[3,384,6144]{2,1,0:T(8,128)} %get-tuple-element.13, f32[3,384]{1,0:T(4,128)S(1)} %broadcast_maximum_fusion, pred[384,6144]{1,0:T(8,128)(4,1)S(1)} %compare_or_fusion, f32[384,3]{0,1:T(4,128)S(1)} %bitcast.46), kind=kOutput, calls=%fused_computation.28 | convolution fusion | flops 1847623680 | bytes 35693568 | tf_op jit(solution)/shard_map/hrn,nhd->hrd/dot_general | solution.py:67
  297.2 3.2 collective-permute-start.2
  300.4 4.8 %collective-permute-done.2 = bf16[384,384]{0,1:T(8,128)(2,1)S(1)} collective-permute-done((bf16[384,384]{0,1:T(8,128)(2,1)S(1)}, bf16[384,384]{0,1:T(8,128)(2,1)S(1)}, u32[]{:S(2)}, u32[]{:S(2)}) %collective-permute-start.2) | collective-permute-done | bytes 294944 | tf_op jit(solution)/shard_map/ppermute | solution.py:21
  305.2 0.0 copy-done
  305.2 4.2 %convolution_convert_fusion = bf16[384,5120]{1,0:T(8,128)(2,1)} fusion(bf16[384,384]{0,1:T(8,128)(2,1)S(1)} %collective-permute-done.2, bf16[1,384,5120]{2,1,0:T(8,128)(2,1)S(1)} %copy-done), kind=kOutput, calls=%fused_computation.13 | convolution fusion | flops 1511915520 | bytes 8159232 | tf_op jit(solution)/shard_map/dot_general | solution.py:80
  309.4 6.3 %copy.15 = bf16[384,5120]{0,1:T(8,128)(2,1)} copy(bf16[384,5120]{1,0:T(8,128)(2,1)} %convolution_convert_fusion) | data formatting | bytes 7864320
  315.7 0.0 reduce-scatter.4.cloned.1.call-update
  315.8 36.9 %reduce-scatter.4.cloned.1.call-done = bf16[640,384]{1,0:T(8,128)(2,1)} async-done(((bf16[5120,384]{1,0:T(8,128)(2,1)}), bf16[640,384]{1,0:T(8,128)(2,1)}) %reduce-scatter.4.cloned.1.call-update) | async-done | bytes 491536
  352.6 1.3 copy.16
  353.9 0.0 copy-done.1
  353.9 0.3 fusion.23
  354.2 2.6 collective-permute-start.3
  356.8 11.0 %collective-permute-done.3 = bf16[384,640]{1,0:T(8,128)(2,1)S(1)} collective-permute-done((bf16[384,640]{1,0:T(8,128)(2,1)S(1)}, bf16[384,640]{1,0:T(8,128)(2,1)S(1)}, u32[]{:S(2)}, u32[]{:S(2)}) %collective-permute-start.3) | collective-permute-done | bytes 491552 | tf_op jit(solution)/shard_map/ppermute | solution.py:17
  367.8 0.8 copy.18
  (6 shorter events, 0.0 us)
Async XLA Ops:
  6.5 104.0 %all-gather.5.cloned.1.call-start = ((), (), s32[]{:S(2)}) async-start(), calls=%async_computation.1 | async-start | bytes 4423680 | tf_op jit(solution)/shard_map/all_gather | solution.py:41
  9.7 10.2 %collective-permute-start = (bf16[384,640]{1,0:T(8,128)(2,1)S(1)}, bf16[384,640]{1,0:T(8,128)(2,1)S(1)}, u32[]{:S(2)}, u32[]{:S(2)}) collective-permute-start(bf16[384,640]{1,0:T(8,128)(2,1)S(1)} %fusion.22), channel_id=1, source_target_pairs={{0,0},{1,8},{8,1},{9,9},{2,2},{3,10},{10,3},{11,11},{4,4},{5,12},{... | collective-permute-start | bytes 1474568 | tf_op jit(solution)/shard_map/ppermute | solution.py:21
  19.9 0.8 copy-start.3
  20.7 165.2 %all-gather.7.cloned.1.call-start = ((), (), s32[]{:S(2)}) async-start(), calls=%async_computation.2 | async-start | bytes 12533760 | tf_op jit(solution)/shard_map/all_gather | solution.py:47
  20.7 13.0 %collective-permute-start.1 = (bf16[320,3,384]{2,0,1:T(8,128)(2,1)}, bf16[320,3,384]{2,0,1:T(8,128)(2,1)S(1)}, u32[]{:S(2)}, u32[]{:S(2)}) collective-permute-start(bf16[320,3,384]{2,0,1:T(8,128)(2,1)} %bitcast.49), channel_id=1, source_target_pairs={{0,0},{1,8},{8,1},{9,9},{2,2},{3,10},{10,3},{11,11},{4,4},{5,12},{... | collective-permute-start | bytes 2211848 | tf_op jit(solution)/shard_map/ppermute | solution.py:21
  33.7 0.9 copy-start.2
  34.6 204.5 %all-gather.9.cloned.1.call-start = ((), (), s32[]{:S(2)}) async-start(), calls=%async_computation.3 | async-start | bytes 5013504 | tf_op jit(solution)/shard_map/all_gather | solution.py:55
  197.7 85.1 %all-gather.11.cloned.1.call-start = ((), (), s32[]{:S(2)}) async-start(), calls=%async_computation.4 | async-start | bytes 5013504 | tf_op jit(solution)/shard_map/all_gather | solution.py:56
  198.2 154.4 %reduce-scatter.4.cloned.1.call-start = ((), (), s32[]{:S(2)}) async-start(), calls=%async_computation.5 | async-start | bytes 4423680
  282.8 22.5 %copy-start = (bf16[1,384,5120]{2,1,0:T(8,128)(2,1)S(1)}, bf16[1,384,5120]{2,1,0:T(8,128)(2,1)}, u32[]{:S(2)}) copy-start(bf16[1,384,5120]{2,1,0:T(8,128)(2,1)} %param.13) | copy-start | bytes 11796484
  297.2 8.0 %collective-permute-start.2 = (bf16[384,384]{0,1:T(8,128)(2,1)S(1)}, bf16[384,384]{0,1:T(8,128)(2,1)S(1)}, u32[]{:S(2)}, u32[]{:S(2)}) collective-permute-start(bf16[384,384]{0,1:T(8,128)(2,1)S(1)} %bitcast.50), channel_id=1, source_target_pairs={{0,0},{1,8},{8,1},{9,9},{2,2},{3,10},{10,3},{11,11},{4,4},{5,12},{... | collective-permute-start | bytes 884744 | tf_op jit(solution)/shard_map/ppermute | solution.py:21
  309.4 44.5 %copy-start.1 = (bf16[1,384,640]{2,1,0:T(8,128)(2,1)S(1)}, bf16[1,384,640]{2,1,0:T(8,128)(2,1)}, u32[]{:S(2)}) copy-start(bf16[1,384,640]{2,1,0:T(8,128)(2,1)} %param.7) | copy-start | bytes 1474564
  354.2 13.5 %collective-permute-start.3 = (bf16[384,640]{1,0:T(8,128)(2,1)S(1)}, bf16[384,640]{1,0:T(8,128)(2,1)S(1)}, u32[]{:S(2)}, u32[]{:S(2)}) collective-permute-start(bf16[384,640]{1,0:T(8,128)(2,1)S(1)} %fusion.23), channel_id=1, source_target_pairs={{0,128},{128,0},{1,129},{129,1},{2,130},{130,2},{3,131},{131,3},{4... | collective-permute-start | bytes 1474568 | tf_op jit(solution)/shard_map/ppermute | solution.py:17
Sparse Core Ops, SparseCore 0:
  20.8 89.7 all-gather.4
  112.4 73.3 all-gather.6
  197.8 41.2 all-gather.8
  240.7 41.9 all-gather.10
  315.9 36.6 reduce-scatter.3
